TPU v7x, 512 devices: a whole 4x4x16 slice. The times are simulated.
512 devices in a mesh: ma: 32 (over z, core), row: 16 (over y, x).
Axes of the slice: x: 4, y: 4, z: 16, core: 2. Of those that a mesh axis runs over, the one named last changes fastest.
Arguments:
- seed_field: bfloat16 [4, 16, 2, 1024, 1024], P(None, 'row', None, 'ma'), may hold values from -6 to 6
- cotangent: bfloat16 [2, 16, 2, 1024, 1024], P(None, 'row', None, 'ma'), may hold values from -6 to 6
- step_size: float32 [1], replicated, may hold values from 0.25 to 1
- owner_list: int32 [1024], replicated, may hold values from 0 to 1023, as said below
Outputs:
- nonlinear: float32 [2, 16, 2, 1024, 1024], P(None, 'row', None, 'ma')
- seed_next: float32 [4, 16, 2, 1024, 1024], P(None, 'row', None, 'ma')
Inputs may be any that keep to these rules, and one draw needn't show every extreme that they name: owner_list is a permutation of the wavenumbers; entries 32 d to 32 (d + 1) - 1 name the wavenumbers of owner d, and a block that holds m also holds 1023 - m.
All inputs are finite; a program needn't handle non-finite values.
Results may differ from a plain program's by a relative error of at most 0.0082.
Values may be sent and summed in bfloat16 or wider, within the bound.
A program may use at most 64 MiB of HBM per device.

v0:
```python
import math
import jax
import jax.numpy as jnp
from jax import lax
from jax.sharding import PartitionSpec as P

WAVES = 1024
DEGREES = 1024
NLAT = 1024
NLON = 2048


def with_halo(cells, sides, width):
    for axis, dim in sides:
        count = lax.axis_size(axis)
        ends = count - 1
        head = lax.slice_in_dim(cells, 0, width, axis=dim)
        tail = lax.slice_in_dim(cells, cells.shape[dim] - width, cells.shape[dim], axis=dim)
        cells = jnp.concatenate(
            [
                lax.ppermute(tail, axis, [(i, (i + 1) % count) for i in range(ends)]),
                cells,
                lax.ppermute(head, axis, [((i + 1) % count, i) for i in range(ends)]),
            ],
            axis=dim,
        )
    return cells


def lat_cosines(theta_index):
    degree = jnp.arange(DEGREES, dtype=jnp.int32)
    phase_index = (2 * theta_index[:, None] + 1) * degree[None, :] % (4 * NLAT)
    return jnp.cos(phase_index.astype(jnp.float32) * (math.pi / (2 * NLAT))).astype(jnp.bfloat16)


def wave_cosines(wave_ids):
    points = jnp.arange(NLON, dtype=jnp.int32)
    phase_index = wave_ids[:, None] * points[None, :] % NLON
    angles = phase_index.astype(jnp.float32) * (2.0 * math.pi / NLON)
    return jnp.stack([jnp.cos(angles), -jnp.sin(angles)]).astype(jnp.bfloat16)


def local(seed_field, cotangent, step_size, owner_list):
    own_waves = cotangent.shape[3]
    norm_scale = 2.0 / math.sqrt(DEGREES * WAVES)
    block_width = min(128, WAVES)
    my_waves = lax.dynamic_slice_in_dim(owner_list, lax.axis_index("ma") * own_waves, own_waves)
    degree = jnp.arange(DEGREES, dtype=jnp.int32)
    live_cols = degree[:, None] >= my_waves[None, :]
    live_rows = jnp.transpose(live_cols)
    zero_value = jnp.zeros((), jnp.bfloat16)
    listed = jnp.take(seed_field, owner_list, axis=4)
    owned_seed = lax.all_to_all(listed, "ma", split_axis=4, concat_axis=3, tiled=True)
    lat_table = lat_cosines(jnp.arange(NLAT, dtype=jnp.int32))
    forward_rows = jnp.einsum(
        "crslk,tl->crstk",
        jnp.where(live_cols, owned_seed, zero_value),
        lat_table,
        preferred_element_type=jnp.float32,
    )
    adjoint_rows = jnp.einsum(
        "crskl,tl->crstk",
        jnp.where(live_rows, cotangent, zero_value),
        lat_table,
        preferred_element_type=jnp.float32,
    )
    spec_rows = jnp.concatenate([forward_rows, adjoint_rows], axis=0).astype(jnp.bfloat16)
    gridded = lax.all_to_all(spec_rows, "ma", split_axis=3, concat_axis=4, tiled=True)
    grid_field = None
    for start in range(0, WAVES, block_width):
        wave_block = wave_cosines(owner_list[start : start + block_width])
        partial_grid = jnp.einsum(
            "crsjm,smf->crjf",
            gridded[..., start : start + block_width],
            wave_block,
            preferred_element_type=jnp.float32,
        )
        grid_field = partial_grid if grid_field is None else grid_field + partial_grid
    grid_field = norm_scale * grid_field
    radial_pair = jnp.stack([grid_field[1], grid_field[3]])
    padded = with_halo(radial_pair, (("row", 1),), 1)
    slopes = 0.5 * (padded[:, 2:] - padded[:, :-2])
    vel_tor = grid_field[0]
    mag_tor = grid_field[2]
    adj_vel = grid_field[4]
    adj_mag = grid_field[5]
    vel_pol = slopes[0]
    mag_pol = slopes[1]
    term_vel = mag_tor * mag_pol - vel_tor * vel_pol
    term_mag = vel_tor * mag_pol - vel_pol * mag_tor
    grad_vtor = -vel_pol * adj_vel + mag_pol * adj_mag
    grad_vpol = -vel_tor * adj_vel - mag_tor * adj_mag
    grad_mtor = mag_pol * adj_vel - vel_pol * adj_mag
    grad_mpol = mag_tor * adj_vel + vel_tor * adj_mag
    cotangent_pair = jnp.stack([grad_vpol, grad_mpol])
    padded_back = with_halo(cotangent_pair, (("row", 1),), 1)
    back_slopes = 0.5 * (padded_back[:, :-2] - padded_back[:, 2:])
    analysis_in = jnp.stack(
        [term_vel, term_mag, grad_vtor, back_slopes[0], grad_mtor, back_slopes[1]]
    ).astype(jnp.bfloat16)
    spectra_parts = []
    for start in range(0, WAVES, block_width):
        wave_block = wave_cosines(owner_list[start : start + block_width])
        spectra_parts.append(
            jnp.einsum(
                "crjf,smf->crsjm", analysis_in, wave_block, preferred_element_type=jnp.float32
            )
        )
    spectra = (norm_scale * jnp.concatenate(spectra_parts, axis=4)).astype(jnp.bfloat16)
    position = jnp.arange(NLAT, dtype=jnp.int32)
    returned = lax.all_to_all(spectra, "ma", split_axis=4, concat_axis=3, tiled=True)
    back_table = lat_cosines(position)
    result = jnp.einsum("crstk,tl->crskl", returned, back_table, preferred_element_type=jnp.float32)
    result = jnp.where(live_rows, result, 0.0)
    nonlinear = result[:2]
    seed_next = jnp.swapaxes(owned_seed, 3, 4).astype(jnp.float32) - step_size[0] * result[2:]
    return (nonlinear, seed_next)


def solution(mesh):
    return jax.shard_map(
        local,
        mesh=mesh,
        in_specs=(P(None, "row", None, "ma", None), P(None, "row", None, "ma", None), P(), P()),
        out_specs=(P(None, "row", None, "ma", None), P(None, "row", None, "ma", None)),
        check_vma=False,
    )
```

profile of v0, /device:TPU:15, one launch (start us, length us, event | category | flops | bytes accessed | tf_op | source)
XLA Modules:
  0.0 314.3 jit_solution(7844892380250730172)
XLA Ops:
  0.6 0.7 compare_and_fusion
  1.3 0.7 fusion.140
  2.0 2.8 copy.26
  4.9 8.9 %gather_fusion = bf16[1024,4,2,32]{3,1,2,0:T(4,128)(2,1)} fusion(bf16[4,2,32,1024]{2,0,3,1:T(4,128)(2,1)S(1)} %bitcast.362, s32[1024]{0:T(1024)S(1)} %fusion.140), kind=kCustom, calls=%fused_computation | custom fusion | bytes 1052672 | tf_op jit(solution)/shard_map/jit(_take)/gather | solution.py:52
  13.7 5.2 %fusion.173 = bf16[1024,1,2,4,32]{4,3,2,1,0:T(4,128)(2,1)S(1)} fusion(bf16[1024,4,2,32]{3,1,2,0:T(4,128)(2,1)} %gather_fusion, pred[1024]{0:T(1024)(128)(4,1)S(1)} %compare_and_fusion), kind=kLoop, calls=%fused_computation.271 | loop fusion | flops 262144 | bytes 1049600
  19.0 2.7 reshape.1275
  21.7 16.6 %all-to-all-start = ((bf16[32,2,4096]{2,1,0:T(2,128)(2,1)}), bf16[32,2,4096]{2,1,0:T(2,128)(2,1)S(1)}, u32[]{:S(2)}, u32[]{:S(2)}) async-start(bf16[32,2,4096]{2,1,0:T(2,128)(2,1)} %reshape.1275), calls=%async_computation | async-start | bytes 1048576 | tf_op jit(solution)/shard_map/all_to_all | solution.py:53
  38.5 16.2 %fusion.45 = bf16[2,1,2,1024,32]{3,4,2,0,1:T(8,128)(2,1)S(1)} fusion(s32[1024]{0:T(1024)S(1)} %multiply_add_fusion.1, bf16[2,1,2,32,1024]{4,3,2,1,0:T(8,128)(2,1)S(1)} %copy-done.18, pred[32,1024]{1,0:T(8,128)(4,1)S(1)} %iota_compare_fusion.1), kind=kOutput, calls=%fused_computation.75 | convolution fusion | flops 284426240 | bytes 561152 | tf_op jit(solution)/shard_map/crskl,tl->crstk/dot_general | solution.py:61
  54.7 16.9 %all-to-all-done = bf16[32,2,4096]{2,1,0:T(2,128)(2,1)S(1)} async-done(((bf16[32,2,4096]{2,1,0:T(2,128)(2,1)}), bf16[32,2,4096]{2,1,0:T(2,128)(2,1)S(1)}, u32[]{:S(2)}, u32[]{:S(2)}) %all-to-all-start) | async-done | bytes 524320 | tf_op jit(solution)/shard_map/all_to_all | solution.py:53
  71.6 1.0 reshape.1276
  72.7 4.0 %fusion.171 = (f32[4,1,2,32,32,32]{4,3,5,2,0,1:T(8,128)}, bf16[4,1,2,32,32,32]{4,3,5,2,0,1:T(8,128)(2,1)}) fusion(bf16[4,1,2,32,32,32]{3,0,2,5,4,1:T(4,128)(2,1)S(1)} %bitcast.361), kind=kLoop, calls=%fused_computation.269 | loop fusion | flops 262144 | bytes 2097152 | tf_op jit(solution)/shard_map/convert_element_type | solution.py:116
  76.7 3.5 %all_to_all.40 = bf16[4,2,1024,32]{2,3,1,0:T(8,128)(2,1)S(1)} reshape(bf16[4,1,2,32,32,32]{4,3,5,2,0,1:T(8,128)(2,1)} %get-tuple-element.11) | data formatting | bytes 1048576 | tf_op jit(solution)/shard_map/all_to_all | solution.py:53
  80.2 16.3 %fusion.39 = bf16[4,1,2,1024,32]{3,4,2,0,1:T(8,128)(2,1)S(1)} fusion(s32[1024]{0:T(1024)S(1)} %multiply_add_fusion.1, bf16[4,2,1024,32]{2,3,1,0:T(8,128)(2,1)S(1)} %all_to_all.40, pred[1024,32]{0,1:T(8,128)(4,1)S(1)} %iota_compare_fusion), kind=kOutput, calls=%fused_computation.73 | convolution fusion | flops 553123840 | bytes 1085440 | tf_op jit(solution)/shard_map/crslk,tl->crstk/dot_general | solution.py:55
  96.5 0.9 pad_maximum_fusion.8
  97.5 6.8 %copy.29 = bf16[6,1,2,1024,32]{4,2,0,1,3:T(2,128)(2,1)S(1)} copy(bf16[6,1,2,1024,32]{3,4,2,0,1:T(8,128)(2,1)} %pad_maximum_fusion.8) | data formatting | bytes 1572864 | tf_op jit(solution)/shard_map/concatenate | solution.py:67
  104.3 3.7 %reshape.1277 = bf16[32,2,6144]{2,1,0:T(2,128)(2,1)} reshape(bf16[1024,1,6,2,32]{4,3,2,1,0:T(2,128)(2,1)S(1)} %bitcast.359) | data formatting | bytes 1572864
  108.0 5.1 %all-to-all-start.1 = ((bf16[32,2,6144]{2,1,0:T(2,128)(2,1)}), bf16[32,2,6144]{2,1,0:T(2,128)(2,1)}, u32[]{:S(2)}, u32[]{:S(2)}) async-start(bf16[32,2,6144]{2,1,0:T(2,128)(2,1)} %reshape.1277), calls=%async_computation.1 | async-start | bytes 1572864 | tf_op jit(solution)/shard_map/all_to_all | solution.py:68
  113.1 9.9 %cosine_convert_fusion.6 = (bf16[1,128,2048]{2,1,0:T(8,128)(2,1)}, bf16[1,128,2048]{2,1,0:T(8,128)(2,1)}, bf16[1,128,2048]{2,1,0:T(8,128)(2,1)}, bf16[1,128,2048]{2,1,0:T(8,128)(2,1)}) fusion(s32[128]{0:T(128)S(1)} %get-tuple-element.19, s32[128]{0:T(128)S(1)} %get-tuple-element.16), kind=kLoop, calls=%fused_computation.169 | loop fusion | flops 8912896 | bytes 2098176 | tf_op jit(solution)/shard_map/convert.28
  123.0 9.9 %cosine_convert_fusion.4 = (bf16[1,128,2048]{2,1,0:T(8,128)(2,1)}, bf16[1,128,2048]{2,1,0:T(8,128)(2,1)}, bf16[1,128,2048]{2,1,0:T(8,128)(2,1)}, bf16[1,128,2048]{2,1,0:T(8,128)(2,1)}) fusion(s32[128]{0:T(128)S(1)} %get-tuple-element.17, s32[128]{0:T(128)S(1)} %get-tuple-element.18), kind=kLoop, calls=%fused_computation.161 | loop fusion | flops 8912896 | bytes 2098176 | tf_op jit(solution)/shard_map/convert.24
  132.8 9.8 %cosine_convert_fusion.2 = (bf16[1,128,2048]{2,1,0:T(8,128)(2,1)}, bf16[1,128,2048]{2,1,0:T(8,128)(2,1)}, bf16[1,128,2048]{2,1,0:T(8,128)(2,1)}, bf16[1,128,2048]{2,1,0:T(8,128)(2,1)}) fusion(s32[128]{0:T(128)S(1)} %get-tuple-element.21, s32[128]{0:T(128)S(1)} %get-tuple-element.20), kind=kLoop, calls=%fused_computation.153 | loop fusion | flops 8912896 | bytes 2098176 | tf_op jit(solution)/shard_map/convert.20
  142.7 9.8 %cosine_convert_fusion = (bf16[1,128,2048]{2,1,0:T(8,128)(2,1)}, bf16[1,128,2048]{2,1,0:T(8,128)(2,1)}, bf16[1,128,2048]{2,1,0:T(8,128)(2,1)}, bf16[1,128,2048]{2,1,0:T(8,128)(2,1)}) fusion(s32[128]{0:T(128)S(1)} %get-tuple-element.22, s32[128]{0:T(128)S(1)} %get-tuple-element.23), kind=kLoop, calls=%fused_computation.145 | loop fusion | flops 8912896 | bytes 2098176 | tf_op jit(solution)/shard_map/convert.16
  152.5 5.1 %all-to-all-done.1 = bf16[32,2,6144]{2,1,0:T(2,128)(2,1)} async-done(((bf16[32,2,6144]{2,1,0:T(2,128)(2,1)}), bf16[32,2,6144]{2,1,0:T(2,128)(2,1)}, u32[]{:S(2)}, u32[]{:S(2)}) %all-to-all-start.1) | async-done | bytes 786464 | tf_op jit(solution)/shard_map/all_to_all | solution.py:68
  157.6 7.2 %reshape.1278 = bf16[1024,1,6,2,32]{4,3,2,1,0:T(2,128)(2,1)S(1)} reshape(bf16[32,2,6144]{2,1,0:T(2,128)(2,1)} %all-to-all-done.1) | data formatting | bytes 1572864
  164.8 3.7 %copy.58 = bf16[6,1,2,32,32,32]{5,3,4,2,0,1:T(8,128)(2,1)} copy(bf16[6,1,2,32,32,32]{5,2,0,4,3,1:T(2,128)(2,1)S(1)} %bitcast.355) | data formatting | bytes 1572864 | tf_op jit(solution)/shard_map/all_to_all | solution.py:68
  168.5 5.3 %all_to_all.44 = bf16[6,1,2,32,1024]{4,3,2,0,1:T(8,128)(2,1)S(1)} reshape(bf16[6,1,2,32,32,32]{5,4,3,2,0,1:T(8,128)(2,1)} %bitcast.356) | data formatting | bytes 1572864 | tf_op jit(solution)/shard_map/all_to_all | solution.py:68
  174.3 0.6 copy-done.11
  178.9 0.8 fusion.15
  179.7 3.1 collective-permute-start.1
  182.9 2.2 collective-permute-start
  185.1 2.5 collective-permute-start.3
  187.6 4.9 %collective-permute-start.2 = (f32[2,1,32,2048]{3,2,1,0:T(8,128)S(1)}, f32[2,1,32,2048]{3,2,1,0:T(8,128)S(1)}, u32[]{:S(2)}, u32[]{:S(2)}) collective-permute-start(f32[2,1,32,2048]{3,2,1,0:T(8,128)S(1)} %pad_maximum_fusion.26), channel_id=1, source_target_pairs={{0,1},{1,2},{2,3},{3,4},{4,5},{5,6},{6,7},{7,8},{8,9},{9,10},{10,1... | collective-permute-start | bytes 1572872 | tf_op jit(solution)/shard_map/ppermute | solution.py:21
  192.6 1.5 collective-permute-done.1
  194.1 5.0 %collective-permute-done = f32[2,1,32,2048]{3,2,1,0:T(8,128)S(1)} collective-permute-done((f32[2,1,32,2048]{3,2,1,0:T(8,128)S(1)}, f32[2,1,32,2048]{3,2,1,0:T(8,128)S(1)}, u32[]{:S(2)}, u32[]{:S(2)}) %collective-permute-start) | collective-permute-done | bytes 524320 | tf_op jit(solution)/shard_map/ppermute | solution.py:23
  199.3 11.0 %collective-permute-done.3 = f32[2,1,32,2048]{3,2,1,0:T(8,128)S(1)} collective-permute-done((f32[2,1,32,2048]{3,2,1,0:T(8,128)S(1)}, f32[2,1,32,2048]{3,2,1,0:T(8,128)S(1)}, u32[]{:S(2)}, u32[]{:S(2)}) %collective-permute-start.3) | collective-permute-done | bytes 524320 | tf_op jit(solution)/shard_map/ppermute | solution.py:23
  210.9 0.5 fusion.54
  211.4 0.5 fusion.53
  214.5 1.0 multiply_convert_fusion
  215.5 6.8 %copy.31 = bf16[6,1,2,32,1024]{3,2,1,0,4:T(2,128)(2,1)S(1)} copy(bf16[6,1,2,32,1024]{4,3,0,2,1:T(8,128)(2,1)} %multiply_convert_fusion) | data formatting | bytes 1572864 | tf_op jit(solution)/shard_map/convert_element_type | solution.py:109
  222.4 3.7 %reshape.1279 = bf16[32,2,6144]{2,1,0:T(2,128)(2,1)} reshape(bf16[1024,6,1,2,32]{4,3,2,1,0:T(2,128)(2,1)S(1)} %bitcast.360) | data formatting | bytes 1572864
  226.1 9.4 %all-to-all-start.2 = ((bf16[32,2,6144]{2,1,0:T(2,128)(2,1)}), bf16[32,2,6144]{2,1,0:T(2,128)(2,1)}, u32[]{:S(2)}, u32[]{:S(2)}) async-start(bf16[32,2,6144]{2,1,0:T(2,128)(2,1)} %reshape.1279), calls=%async_computation.2 | async-start | bytes 1572864 | tf_op jit(solution)/shard_map/all_to_all | solution.py:111
  236.2 4.6 %reshape.1245 = f32[4,1,2,1024,32]{3,4,2,0,1:T(8,128)} reshape(f32[4,1,2,32,32,32]{4,3,5,2,0,1:T(8,128)} %get-tuple-element.10) | data formatting | bytes 2097152 | tf_op jit(solution)/shard_map/convert_element_type | solution.py:116
  240.7 39.3 %all-to-all-done.2 = bf16[32,2,6144]{2,1,0:T(2,128)(2,1)} async-done(((bf16[32,2,6144]{2,1,0:T(2,128)(2,1)}), bf16[32,2,6144]{2,1,0:T(2,128)(2,1)}, u32[]{:S(2)}, u32[]{:S(2)}) %all-to-all-start.2) | async-done | bytes 786464 | tf_op jit(solution)/shard_map/all_to_all | solution.py:111
  280.0 7.2 %reshape.1280 = bf16[1024,6,1,2,32]{4,3,2,1,0:T(2,128)(2,1)S(1)} reshape(bf16[32,2,6144]{2,1,0:T(2,128)(2,1)} %all-to-all-done.2) | data formatting | bytes 1572864
  287.2 3.7 %copy.57 = bf16[6,1,2,32,32,32]{3,4,5,2,0,1:T(8,128)(2,1)} copy(bf16[6,1,2,32,32,32]{3,2,0,5,4,1:T(2,128)(2,1)S(1)} %bitcast.357) | data formatting | bytes 1572864 | tf_op jit(solution)/shard_map/all_to_all | solution.py:111
  290.9 5.0 %reshape.1244 = bf16[6,2,1024,32]{2,3,1,0:T(8,128)(2,1)S(1)} reshape(bf16[6,1,2,32,32,32]{4,3,5,2,0,1:T(8,128)(2,1)} %bitcast.358) | data formatting | bytes 1572864 | tf_op jit(solution)/shard_map/reshape.39
  296.0 16.2 %fusion.33 = f32[6,2,32,1024]{3,2,1,0:T(8,128)S(1)} fusion(bf16[6,2,1024,32]{2,3,1,0:T(8,128)(2,1)S(1)} %reshape.1244, s32[1024]{0:T(1024)S(1)} %multiply_add_fusion.1, pred[32,1024]{1,0:T(8,128)(4,1)S(1)} %iota_compare_fusion.1), kind=kOutput, calls=%fused_computation.71 | convolution fusion | flops 821428224 | bytes 2396160 | tf_op jit(solution)/shard_map/crstk,tl->crskl/dot_general | solution.py:113
  312.1 0.8 slice_bitcast_fusion
  312.9 1.1 fusion.82
  (68 shorter events, 8.2 us)
Async XLA Ops:
  19.0 19.3 %copy-start.17 = (s32[1024]{0:T(1024)S(1)}, s32[1024]{0:T(1024)}, u32[]{:S(2)}) copy-start(s32[1024]{0:T(1024)} %param.7) | copy-start | bytes 12292
  19.0 19.6 %copy-start.18 = (bf16[2,1,2,32,1024]{4,3,2,1,0:T(8,128)(2,1)S(1)}, bf16[2,1,2,32,1024]{4,3,2,1,0:T(8,128)(2,1)}, u32[]{:S(2)}) copy-start(bf16[2,1,2,32,1024]{4,3,2,1,0:T(8,128)(2,1)} %param.5) | copy-start | bytes 786436
  21.7 50.0 %all-to-all-start = ((bf16[32,2,4096]{2,1,0:T(2,128)(2,1)}), bf16[32,2,4096]{2,1,0:T(2,128)(2,1)S(1)}, u32[]{:S(2)}, u32[]{:S(2)}) async-start(bf16[32,2,4096]{2,1,0:T(2,128)(2,1)} %reshape.1275), calls=%async_computation | async-start | bytes 1048576 | tf_op jit(solution)/shard_map/all_to_all | solution.py:53
  108.0 49.6 %all-to-all-start.1 = ((bf16[32,2,6144]{2,1,0:T(2,128)(2,1)}), bf16[32,2,6144]{2,1,0:T(2,128)(2,1)}, u32[]{:S(2)}, u32[]{:S(2)}) async-start(bf16[32,2,6144]{2,1,0:T(2,128)(2,1)} %reshape.1277), calls=%async_computation.1 | async-start | bytes 1572864 | tf_op jit(solution)/shard_map/all_to_all | solution.py:68
  168.5 5.3 %copy-start.3 = (bf16[1,128,2048]{2,1,0:T(8,128)(2,1)S(1)}, bf16[1,128,2048]{2,1,0:T(8,128)(2,1)}, u32[]{:S(2)}) copy-start(bf16[1,128,2048]{2,1,0:T(8,128)(2,1)} %get-tuple-element.38) | copy-start | bytes 1572868
  168.5 5.4 %copy-start.4 = (bf16[1,128,2048]{2,1,0:T(8,128)(2,1)S(1)}, bf16[1,128,2048]{2,1,0:T(8,128)(2,1)}, u32[]{:S(2)}) copy-start(bf16[1,128,2048]{2,1,0:T(8,128)(2,1)} %get-tuple-element.39) | copy-start | bytes 1572868
  173.8 1.0 copy-start.11
  173.8 1.2 copy-start.12
  173.9 1.6 copy-start.1
  173.9 1.6 copy-start.2
  175.0 1.1 copy-start.9
  175.0 1.3 copy-start.10
  175.4 1.2 copy-start.5
  175.5 1.3 copy-start.6
  176.3 1.1 copy-start.13
  176.3 1.3 copy-start.14
  176.7 1.2 copy-start.7
  176.7 1.3 copy-start.8
  177.6 1.1 copy-start.15
  177.6 1.3 copy-start.16
  179.7 14.3 %collective-permute-start.1 = (f32[2,1,32,2048]{3,2,1,0:T(8,128)S(1)}, f32[2,1,32,2048]{3,2,1,0:T(8,128)S(1)}, u32[]{:S(2)}, u32[]{:S(2)}) collective-permute-start(f32[2,1,32,2048]{3,2,1,0:T(8,128)S(1)} %pad_maximum_fusion.25), channel_id=1, source_target_pairs={{0,1},{1,2},{2,3},{3,4},{4,5},{5,6},{6,7},{7,8},{8,9},{9,10},{10,1... | collective-permute-start | bytes 1572872 | tf_op jit(solution)/shard_map/ppermute | solution.py:21
  182.9 16.2 %collective-permute-start = (f32[2,1,32,2048]{3,2,1,0:T(8,128)S(1)}, f32[2,1,32,2048]{3,2,1,0:T(8,128)S(1)}, u32[]{:S(2)}, u32[]{:S(2)}) collective-permute-start(f32[2,1,32,2048]{3,2,1,0:T(8,128)S(1)} %pad_maximum_fusion.25), channel_id=1, source_target_pairs={{1,0},{2,1},{3,2},{4,3},{5,4},{6,5},{7,6},{8,7},{9,8},{10,9},{11,1... | collective-permute-start | bytes 1572872 | tf_op jit(solution)/shard_map/ppermute | solution.py:23
  185.1 25.1 %collective-permute-start.3 = (f32[2,1,32,2048]{3,2,1,0:T(8,128)S(1)}, f32[2,1,32,2048]{3,2,1,0:T(8,128)S(1)}, u32[]{:S(2)}, u32[]{:S(2)}) collective-permute-start(f32[2,1,32,2048]{3,2,1,0:T(8,128)S(1)} %pad_maximum_fusion.26), channel_id=1, source_target_pairs={{1,0},{2,1},{3,2},{4,3},{5,4},{6,5},{7,6},{8,7},{9,8},{10,9},{11,1... | collective-permute-start | bytes 1572872 | tf_op jit(solution)/shard_map/ppermute | solution.py:23
  187.6 22.6 %collective-permute-start.2 = (f32[2,1,32,2048]{3,2,1,0:T(8,128)S(1)}, f32[2,1,32,2048]{3,2,1,0:T(8,128)S(1)}, u32[]{:S(2)}, u32[]{:S(2)}) collective-permute-start(f32[2,1,32,2048]{3,2,1,0:T(8,128)S(1)} %pad_maximum_fusion.26), channel_id=1, source_target_pairs={{0,1},{1,2},{2,3},{3,4},{4,5},{5,6},{6,7},{7,8},{8,9},{9,10},{10,1... | collective-permute-start | bytes 1572872 | tf_op jit(solution)/shard_map/ppermute | solution.py:21
  226.1 53.9 %all-to-all-start.2 = ((bf16[32,2,6144]{2,1,0:T(2,128)(2,1)}), bf16[32,2,6144]{2,1,0:T(2,128)(2,1)}, u32[]{:S(2)}, u32[]{:S(2)}) async-start(bf16[32,2,6144]{2,1,0:T(2,128)(2,1)} %reshape.1279), calls=%async_computation.2 | async-start | bytes 1572864 | tf_op jit(solution)/shard_map/all_to_all | solution.py:111
  295.9 17.0 %copy-start = (f32[4,1,2,1024,32]{3,4,2,0,1:T(8,128)S(1)}, f32[4,1,2,1024,32]{3,4,2,0,1:T(8,128)}, u32[]{:S(2)}) copy-start(f32[4,1,2,1024,32]{3,4,2,0,1:T(8,128)} %reshape.1245) | copy-start | bytes 3145732
where the time goes:
time: 319 us; the launch traced here: 314 us
  local copies, waits for them, and re-layouts  79.9 us (25%)
  waiting for transfers between devices  78.8 us (25%)
  matrix products  56.2 us (18%)
  other arithmetic  53.7 us (17%)
  starting transfers between devices  43.7 us (14%)
    another operation x5, other arithmetic  39.4 us
    all_to_all x1, waiting for transfers between devices, local(): lax.all_to_all(spectra, 'ma', split_axis=4, concat_axis=3, tiled=True)  39.3 us
    unnamed x47, local copies, waits for them, and re-layouts  31.5 us
    all_to_all x1, waiting for transfers between devices, local(): lax.all_to_all(listed, 'ma', split_axis=4, concat_axis=3, tiled=True)  16.9 us
    all_to_all x1, starting transfers between devices, local(): lax.all_to_all(listed, 'ma', split_axis=4, concat_axis=3, tiled=True)  16.6 us
    dot_general x1, matrix products, local(): jnp.einsum('crslk,tl->crstk', jnp.where(live_cols, owned_seed, zero_value...  16.3 us
    dot_general x1, matrix products, local(): jnp.einsum('crskl,tl->crstk', jnp.where(live_rows, cotangent, zero_value)...  16.2 us
    dot_general x1, matrix products, local(): jnp.einsum('crstk,tl->crskl', returned, back_table, preferred_element_typ...  16.2 us
  transfers between devices with their start and end apart: 7, of which 6 were waited for; matrix products, arithmetic and copies ran while one was open for 19% of the time, Pallas kernels for 0%

commit v1 on v0

--- a/solution.py
+++ b/solution.py
@@ -65,7 +65,10 @@
         preferred_element_type=jnp.float32,
     )
     spec_rows = jnp.concatenate([forward_rows, adjoint_rows], axis=0).astype(jnp.bfloat16)
-    gridded = lax.all_to_all(spec_rows, "ma", split_axis=3, concat_axis=4, tiled=True)
+    gridded = jnp.concatenate(
+        lax.all_to_all(jnp.stack(jnp.split(spec_rows, lax.axis_size("ma"), axis=3)), "ma", 0, 0),
+        axis=4,
+    )
     grid_field = None
     for start in range(0, WAVES, block_width):
         wave_block = wave_cosines(owner_list[start : start + block_width])

time: 319 us -> 312 us (0.978)
  local copies, waits for them, and re-layouts: 79.9 us -> 71.5 us
    reshape x0 -> x3, local copies, waits for them, and re-layouts: none -> 13.1 us  [local(): jnp.concatenate(lax.all_to_all(jnp.stack(jnp.split(spec_rows, lax.axis_si...]
    all_to_all x2 -> x0, local copies, waits for them, and re-layouts: 9 us -> none  [local(): lax.all_to_all(spec_rows, 'ma', split_axis=3, concat_axis=4, tiled=True)]
    concatenate x1 -> x0, local copies, waits for them, and re-layouts: 6.79 us -> none  [local(): jnp.concatenate([forward_rows, adjoint_rows], axis=0).astype(jnp.bfloat16)]
    unnamed x47, local copies, waits for them, and re-layouts: 31.5 us -> 25.8 us
    unnamed x6 -> x37, other arithmetic: 6.59 us -> 9.6 us
    another operation x5 -> x6, other arithmetic: 39.4 us -> 39.5 us
  transfers between devices with their start and end apart: 7 -> 7, of which waited for: 6 -> 6; matrix products, arithmetic and copies ran while one was open for 19% -> 20% of each run, Pallas kernels for 0% -> 0%
where the time goes in v1:
time: 312 us; the launch traced here: 308 us
  waiting for transfers between devices  79.1 us (25%)
  local copies, waits for them, and re-layouts  71.5 us (23%)
  matrix products  56.2 us (18%)
  other arithmetic  55.9 us (18%)
  starting transfers between devices  42.8 us (14%)
    all_to_all x1, waiting for transfers between devices, local(): lax.all_to_all(spectra, 'ma', split_axis=4, concat_axis=3, tiled=True)  39.5 us
    another operation x5, other arithmetic  39.4 us
    unnamed x47, local copies, waits for them, and re-layouts  25.8 us
    all_to_all x1, waiting for transfers between devices, local(): lax.all_to_all(listed, 'ma', split_axis=4, concat_axis=3, tiled=True)  16.9 us
    all_to_all x1, starting transfers between devices, local(): lax.all_to_all(listed, 'ma', split_axis=4, concat_axis=3, tiled=True)  16.6 us
    dot_general x1, matrix products, local(): jnp.einsum('crslk,tl->crstk', jnp.where(live_cols, owned_seed, zero_value...  16.3 us
    dot_general x1, matrix products, local(): jnp.einsum('crskl,tl->crstk', jnp.where(live_rows, cotangent, zero_value)...  16.2 us
    dot_general x1, matrix products, local(): jnp.einsum('crstk,tl->crskl', returned, back_table, preferred_element_typ...  16.1 us
  transfers between devices with their start and end apart: 7, of which 6 were waited for; matrix products, arithmetic and copies ran while one was open for 20% of the time, Pallas kernels for 0%

profile of v1, /device:TPU:15, one launch (start us, length us, event | category | flops | bytes accessed | tf_op | source)
XLA Modules:
  0.0 307.7 jit_solution(15249829411751887190)
XLA Ops:
  0.6 0.7 compare_and_fusion
  1.3 0.7 fusion.173
  2.0 2.8 copy.24
  4.9 8.9 %gather_fusion = bf16[1024,4,2,32]{3,1,2,0:T(4,128)(2,1)} fusion(bf16[4,2,32,1024]{2,0,3,1:T(4,128)(2,1)S(1)} %bitcast.425, s32[1024]{0:T(1024)S(1)} %fusion.173), kind=kCustom, calls=%fused_computation | custom fusion | bytes 1052672 | tf_op jit(solution)/shard_map/jit(_take)/gather | solution.py:52
  13.7 5.3 %fusion.206 = bf16[1024,1,2,4,32]{4,3,2,1,0:T(4,128)(2,1)S(1)} fusion(bf16[1024,4,2,32]{3,1,2,0:T(4,128)(2,1)} %gather_fusion, pred[1024]{0:T(1024)(128)(4,1)S(1)} %compare_and_fusion), kind=kLoop, calls=%fused_computation.397 | loop fusion | flops 262144 | bytes 1049600
  19.0 2.7 reshape.1283
  21.7 16.6 %all-to-all-start = ((bf16[32,2,4096]{2,1,0:T(2,128)(2,1)}), bf16[32,2,4096]{2,1,0:T(2,128)(2,1)S(1)}, u32[]{:S(2)}, u32[]{:S(2)}) async-start(bf16[32,2,4096]{2,1,0:T(2,128)(2,1)} %reshape.1283), calls=%async_computation | async-start | bytes 1048576 | tf_op jit(solution)/shard_map/all_to_all | solution.py:53
  38.6 16.2 %fusion.45 = bf16[2,1,2,1024,32]{3,4,2,0,1:T(8,128)(2,1)S(1)} fusion(s32[1024]{0:T(1024)S(1)} %multiply_add_fusion.1, bf16[2,1,2,32,1024]{4,3,2,1,0:T(8,128)(2,1)S(1)} %copy-done.18, pred[32,1024]{1,0:T(8,128)(4,1)S(1)} %iota_compare_fusion.1), kind=kOutput, calls=%fused_computation.136 | convolution fusion | flops 284426240 | bytes 561152 | tf_op jit(solution)/shard_map/crskl,tl->crstk/dot_general | solution.py:61
  54.8 16.9 %all-to-all-done = bf16[32,2,4096]{2,1,0:T(2,128)(2,1)S(1)} async-done(((bf16[32,2,4096]{2,1,0:T(2,128)(2,1)}), bf16[32,2,4096]{2,1,0:T(2,128)(2,1)S(1)}, u32[]{:S(2)}, u32[]{:S(2)}) %all-to-all-start) | async-done | bytes 524320 | tf_op jit(solution)/shard_map/all_to_all | solution.py:53
  71.7 1.0 reshape.1284
  72.7 4.0 %fusion.204 = (f32[4,1,2,32,32,32]{4,3,5,2,0,1:T(8,128)}, bf16[4,1,2,32,32,32]{4,3,5,2,0,1:T(8,128)(2,1)}) fusion(bf16[4,1,2,32,32,32]{3,0,2,5,4,1:T(4,128)(2,1)S(1)} %bitcast.423), kind=kLoop, calls=%fused_computation.394 | loop fusion | flops 262144 | bytes 2097152 | tf_op jit(solution)/shard_map/convert_element_type | solution.py:119
  76.7 3.5 %all_to_all.30 = bf16[4,2,1024,32]{2,3,1,0:T(8,128)(2,1)S(1)} reshape(bf16[4,1,2,32,32,32]{4,3,5,2,0,1:T(8,128)(2,1)} %get-tuple-element.11) | data formatting | bytes 1048576 | tf_op jit(solution)/shard_map/all_to_all | solution.py:53
  80.2 16.3 %fusion.39 = bf16[4,1,2,1024,32]{3,4,2,0,1:T(8,128)(2,1)S(1)} fusion(s32[1024]{0:T(1024)S(1)} %multiply_add_fusion.1, bf16[4,2,1024,32]{2,3,1,0:T(8,128)(2,1)S(1)} %all_to_all.30, pred[1024,32]{0,1:T(8,128)(4,1)S(1)} %iota_compare_fusion), kind=kOutput, calls=%fused_computation.134 | convolution fusion | flops 553123840 | bytes 1085440 | tf_op jit(solution)/shard_map/crslk,tl->crstk/dot_general | solution.py:55
  99.7 3.7 %reshape.1285 = bf16[32,2,6144]{2,1,0:T(2,128)(2,1)} reshape(bf16[32,1,6,2,32,32]{5,4,3,2,1,0:T(8,128)(2,1)S(1)} %bitcast.424) | data formatting | bytes 1572864
  103.5 4.5 %all-to-all-start.1 = ((bf16[32,2,6144]{2,1,0:T(2,128)(2,1)}), bf16[32,2,6144]{2,1,0:T(2,128)(2,1)S(1)}, u32[]{:S(2)}, u32[]{:S(2)}) async-start(bf16[32,2,6144]{2,1,0:T(2,128)(2,1)} %reshape.1285), calls=%async_computation.1 | async-start | bytes 1572864 | tf_op jit(solution)/shard_map/all_to_all | solution.py:69
  107.9 9.9 %cosine_convert_fusion.6 = (bf16[1,128,2048]{2,1,0:T(8,128)(2,1)}, bf16[1,128,2048]{2,1,0:T(8,128)(2,1)}, bf16[1,128,2048]{2,1,0:T(8,128)(2,1)}, bf16[1,128,2048]{2,1,0:T(8,128)(2,1)}) fusion(s32[128]{0:T(128)S(1)} %get-tuple-element.19, s32[128]{0:T(128)S(1)} %get-tuple-element.16), kind=kLoop, calls=%fused_computation.230 | loop fusion | flops 8912896 | bytes 2098176 | tf_op jit(solution)/shard_map/convert.28
  117.8 9.9 %cosine_convert_fusion.4 = (bf16[1,128,2048]{2,1,0:T(8,128)(2,1)}, bf16[1,128,2048]{2,1,0:T(8,128)(2,1)}, bf16[1,128,2048]{2,1,0:T(8,128)(2,1)}, bf16[1,128,2048]{2,1,0:T(8,128)(2,1)}) fusion(s32[128]{0:T(128)S(1)} %get-tuple-element.17, s32[128]{0:T(128)S(1)} %get-tuple-element.18), kind=kLoop, calls=%fused_computation.222 | loop fusion | flops 8912896 | bytes 2098176 | tf_op jit(solution)/shard_map/convert.24
  127.7 9.8 %cosine_convert_fusion.2 = (bf16[1,128,2048]{2,1,0:T(8,128)(2,1)}, bf16[1,128,2048]{2,1,0:T(8,128)(2,1)}, bf16[1,128,2048]{2,1,0:T(8,128)(2,1)}, bf16[1,128,2048]{2,1,0:T(8,128)(2,1)}) fusion(s32[128]{0:T(128)S(1)} %get-tuple-element.21, s32[128]{0:T(128)S(1)} %get-tuple-element.20), kind=kLoop, calls=%fused_computation.214 | loop fusion | flops 8912896 | bytes 2098176 | tf_op jit(solution)/shard_map/convert.20
  137.5 9.8 %cosine_convert_fusion = (bf16[1,128,2048]{2,1,0:T(8,128)(2,1)}, bf16[1,128,2048]{2,1,0:T(8,128)(2,1)}, bf16[1,128,2048]{2,1,0:T(8,128)(2,1)}, bf16[1,128,2048]{2,1,0:T(8,128)(2,1)}) fusion(s32[128]{0:T(128)S(1)} %get-tuple-element.22, s32[128]{0:T(128)S(1)} %get-tuple-element.23), kind=kLoop, calls=%fused_computation.206 | loop fusion | flops 8912896 | bytes 2098176 | tf_op jit(solution)/shard_map/convert.16
  147.3 5.2 %all-to-all-done.1 = bf16[32,2,6144]{2,1,0:T(2,128)(2,1)S(1)} async-done(((bf16[32,2,6144]{2,1,0:T(2,128)(2,1)}), bf16[32,2,6144]{2,1,0:T(2,128)(2,1)S(1)}, u32[]{:S(2)}, u32[]{:S(2)}) %all-to-all-start.1) | async-done | bytes 786464 | tf_op jit(solution)/shard_map/all_to_all | solution.py:69
  152.6 2.7 reshape.1286
  155.2 2.8 bitcast_bitcast_fusion
  158.0 5.3 %copy.27 = bf16[6,1,2,32,32,32]{5,4,3,2,0,1:T(8,128)(2,1)} copy(bf16[6,1,2,32,32,32]{3,5,2,0,1,4:T(8,128)(2,1)S(1)} %bitcast_bitcast_fusion) | data formatting | bytes 1572864 | tf_op jit(solution)/shard_map/reshape | solution.py:68
  163.3 5.0 %reshape.1243 = bf16[6,1,2,32,1024]{4,3,2,0,1:T(8,128)(2,1)S(1)} reshape(bf16[6,1,2,32,32,32]{5,4,3,2,0,1:T(8,128)(2,1)} %copy.27) | data formatting | bytes 1572864 | tf_op jit(solution)/shard_map/reshape | solution.py:68
  172.3 0.8 fusion.15
  173.2 3.3 %collective-permute-start.1 = (f32[2,1,32,2048]{3,2,1,0:T(8,128)S(1)}, f32[2,1,32,2048]{3,2,1,0:T(8,128)S(1)}, u32[]{:S(2)}, u32[]{:S(2)}) collective-permute-start(f32[2,1,32,2048]{3,2,1,0:T(8,128)S(1)} %pad_maximum_fusion.24), channel_id=1, source_target_pairs={{0,1},{1,2},{2,3},{3,4},{4,5},{5,6},{6,7},{7,8},{8,9},{9,10},{10,1... | collective-permute-start | bytes 1572872 | tf_op jit(solution)/shard_map/ppermute | solution.py:21
  176.5 2.2 collective-permute-start
  178.8 2.4 collective-permute-start.3
  181.2 5.0 %collective-permute-start.2 = (f32[2,1,32,2048]{3,2,1,0:T(8,128)S(1)}, f32[2,1,32,2048]{3,2,1,0:T(8,128)S(1)}, u32[]{:S(2)}, u32[]{:S(2)}) collective-permute-start(f32[2,1,32,2048]{3,2,1,0:T(8,128)S(1)} %pad_maximum_fusion.25), channel_id=1, source_target_pairs={{0,1},{1,2},{2,3},{3,4},{4,5},{5,6},{6,7},{7,8},{8,9},{9,10},{10,1... | collective-permute-start | bytes 1572872 | tf_op jit(solution)/shard_map/ppermute | solution.py:21
  186.2 1.3 collective-permute-done.1
  187.5 5.1 %collective-permute-done = f32[2,1,32,2048]{3,2,1,0:T(8,128)S(1)} collective-permute-done((f32[2,1,32,2048]{3,2,1,0:T(8,128)S(1)}, f32[2,1,32,2048]{3,2,1,0:T(8,128)S(1)}, u32[]{:S(2)}, u32[]{:S(2)}) %collective-permute-start) | collective-permute-done | bytes 524320 | tf_op jit(solution)/shard_map/ppermute | solution.py:23
  192.9 11.0 %collective-permute-done.3 = f32[2,1,32,2048]{3,2,1,0:T(8,128)S(1)} collective-permute-done((f32[2,1,32,2048]{3,2,1,0:T(8,128)S(1)}, f32[2,1,32,2048]{3,2,1,0:T(8,128)S(1)}, u32[]{:S(2)}, u32[]{:S(2)}) %collective-permute-start.3) | collective-permute-done | bytes 524320 | tf_op jit(solution)/shard_map/ppermute | solution.py:23
  204.5 0.5 fusion.54
  205.1 0.5 fusion.53
  207.1 0.5 fusion.49
  207.7 0.5 fusion.48
  208.2 1.0 multiply_convert_fusion
  209.2 6.8 %copy.28 = bf16[6,1,2,32,1024]{3,2,1,0,4:T(2,128)(2,1)S(1)} copy(bf16[6,1,2,32,1024]{4,3,0,2,1:T(8,128)(2,1)} %multiply_convert_fusion) | data formatting | bytes 1572864 | tf_op jit(solution)/shard_map/convert_element_type | solution.py:112
  216.0 3.7 %reshape.1287 = bf16[32,2,6144]{2,1,0:T(2,128)(2,1)} reshape(bf16[1024,6,1,2,32]{4,3,2,1,0:T(2,128)(2,1)S(1)} %bitcast.422) | data formatting | bytes 1572864
  219.8 8.9 %all-to-all-start.2 = ((bf16[32,2,6144]{2,1,0:T(2,128)(2,1)}), bf16[32,2,6144]{2,1,0:T(2,128)(2,1)}, u32[]{:S(2)}, u32[]{:S(2)}) async-start(bf16[32,2,6144]{2,1,0:T(2,128)(2,1)} %reshape.1287), calls=%async_computation.2 | async-start | bytes 1572864 | tf_op jit(solution)/shard_map/all_to_all | solution.py:114
  229.3 4.6 %reshape.1253 = f32[4,1,2,1024,32]{3,4,2,0,1:T(8,128)} reshape(f32[4,1,2,32,32,32]{4,3,5,2,0,1:T(8,128)} %get-tuple-element.10) | data formatting | bytes 2097152 | tf_op jit(solution)/shard_map/convert_element_type | solution.py:119
  233.9 39.5 %all-to-all-done.2 = bf16[32,2,6144]{2,1,0:T(2,128)(2,1)} async-done(((bf16[32,2,6144]{2,1,0:T(2,128)(2,1)}), bf16[32,2,6144]{2,1,0:T(2,128)(2,1)}, u32[]{:S(2)}, u32[]{:S(2)}) %all-to-all-start.2) | async-done | bytes 786464 | tf_op jit(solution)/shard_map/all_to_all | solution.py:114
  273.4 7.2 %reshape.1288 = bf16[1024,6,1,2,32]{4,3,2,1,0:T(2,128)(2,1)S(1)} reshape(bf16[32,2,6144]{2,1,0:T(2,128)(2,1)} %all-to-all-done.2) | data formatting | bytes 1572864
  280.6 3.7 %copy.53 = bf16[6,1,2,32,32,32]{3,4,5,2,0,1:T(8,128)(2,1)} copy(bf16[6,1,2,32,32,32]{3,2,0,5,4,1:T(2,128)(2,1)S(1)} %bitcast.420) | data formatting | bytes 1572864 | tf_op jit(solution)/shard_map/all_to_all | solution.py:114
  284.3 5.0 %reshape.1252 = bf16[6,2,1024,32]{2,3,1,0:T(8,128)(2,1)S(1)} reshape(bf16[6,1,2,32,32,32]{4,3,5,2,0,1:T(8,128)(2,1)} %bitcast.421) | data formatting | bytes 1572864 | tf_op jit(solution)/shard_map/reshape.41
  289.3 16.1 %fusion.33 = f32[6,2,32,1024]{3,2,1,0:T(8,128)S(1)} fusion(bf16[6,2,1024,32]{2,3,1,0:T(8,128)(2,1)S(1)} %reshape.1252, s32[1024]{0:T(1024)S(1)} %multiply_add_fusion.1, pred[32,1024]{1,0:T(8,128)(4,1)S(1)} %iota_compare_fusion.1), kind=kOutput, calls=%fused_computation.132 | convolution fusion | flops 821428224 | bytes 2396160 | tf_op jit(solution)/shard_map/crstk,tl->crskl/dot_general | solution.py:116
  305.5 0.8 slice_bitcast_fusion
  306.3 1.1 fusion.82
  (99 shorter events, 9.7 us)
Async XLA Ops:
  13.7 24.6 %copy-start.17 = (s32[1024]{0:T(1024)S(1)}, s32[1024]{0:T(1024)}, u32[]{:S(2)}) copy-start(s32[1024]{0:T(1024)} %param.7) | copy-start | bytes 12292
  13.7 24.8 %copy-start.18 = (bf16[2,1,2,32,1024]{4,3,2,1,0:T(8,128)(2,1)S(1)}, bf16[2,1,2,32,1024]{4,3,2,1,0:T(8,128)(2,1)}, u32[]{:S(2)}) copy-start(bf16[2,1,2,32,1024]{4,3,2,1,0:T(8,128)(2,1)} %param.5) | copy-start | bytes 786436
  21.7 50.0 %all-to-all-start = ((bf16[32,2,4096]{2,1,0:T(2,128)(2,1)}), bf16[32,2,4096]{2,1,0:T(2,128)(2,1)S(1)}, u32[]{:S(2)}, u32[]{:S(2)}) async-start(bf16[32,2,4096]{2,1,0:T(2,128)(2,1)} %reshape.1283), calls=%async_computation | async-start | bytes 1048576 | tf_op jit(solution)/shard_map/all_to_all | solution.py:53
  103.5 49.1 %all-to-all-start.1 = ((bf16[32,2,6144]{2,1,0:T(2,128)(2,1)}), bf16[32,2,6144]{2,1,0:T(2,128)(2,1)S(1)}, u32[]{:S(2)}, u32[]{:S(2)}) async-start(bf16[32,2,6144]{2,1,0:T(2,128)(2,1)} %reshape.1285), calls=%async_computation.1 | async-start | bytes 1572864 | tf_op jit(solution)/shard_map/all_to_all | solution.py:69
  163.3 5.0 %copy-start.3 = (bf16[1,128,2048]{2,1,0:T(8,128)(2,1)S(1)}, bf16[1,128,2048]{2,1,0:T(8,128)(2,1)}, u32[]{:S(2)}) copy-start(bf16[1,128,2048]{2,1,0:T(8,128)(2,1)} %get-tuple-element.38) | copy-start | bytes 1572868
  163.3 5.0 %copy-start.4 = (bf16[1,128,2048]{2,1,0:T(8,128)(2,1)S(1)}, bf16[1,128,2048]{2,1,0:T(8,128)(2,1)}, u32[]{:S(2)}) copy-start(bf16[1,128,2048]{2,1,0:T(8,128)(2,1)} %get-tuple-element.39) | copy-start | bytes 1572868
  163.3 5.5 %copy-start.11 = (bf16[1,128,2048]{2,1,0:T(8,128)(2,1)S(1)}, bf16[1,128,2048]{2,1,0:T(8,128)(2,1)}, u32[]{:S(2)}) copy-start(bf16[1,128,2048]{2,1,0:T(8,128)(2,1)} %get-tuple-element.40) | copy-start | bytes 1572868
  163.3 5.5 %copy-start.12 = (bf16[1,128,2048]{2,1,0:T(8,128)(2,1)S(1)}, bf16[1,128,2048]{2,1,0:T(8,128)(2,1)}, u32[]{:S(2)}) copy-start(bf16[1,128,2048]{2,1,0:T(8,128)(2,1)} %get-tuple-element.41) | copy-start | bytes 1572868
  168.3 1.0 copy-start.1
  168.3 1.2 copy-start.2
  168.8 1.2 copy-start.9
  168.8 1.3 copy-start.10
  169.2 1.3 copy-start.5
  169.2 1.3 copy-start.6
  169.9 1.2 copy-start.13
  169.9 1.3 copy-start.14
  170.4 1.2 copy-start.7
  170.4 1.3 copy-start.8
  170.9 1.2 copy-start.15
  170.9 1.3 copy-start.16
  173.2 14.3 %collective-permute-start.1 = (f32[2,1,32,2048]{3,2,1,0:T(8,128)S(1)}, f32[2,1,32,2048]{3,2,1,0:T(8,128)S(1)}, u32[]{:S(2)}, u32[]{:S(2)}) collective-permute-start(f32[2,1,32,2048]{3,2,1,0:T(8,128)S(1)} %pad_maximum_fusion.24), channel_id=1, source_target_pairs={{0,1},{1,2},{2,3},{3,4},{4,5},{5,6},{6,7},{7,8},{8,9},{9,10},{10,1... | collective-permute-start | bytes 1572872 | tf_op jit(solution)/shard_map/ppermute | solution.py:21
  176.5 16.2 %collective-permute-start = (f32[2,1,32,2048]{3,2,1,0:T(8,128)S(1)}, f32[2,1,32,2048]{3,2,1,0:T(8,128)S(1)}, u32[]{:S(2)}, u32[]{:S(2)}) collective-permute-start(f32[2,1,32,2048]{3,2,1,0:T(8,128)S(1)} %pad_maximum_fusion.24), channel_id=1, source_target_pairs={{1,0},{2,1},{3,2},{4,3},{5,4},{6,5},{7,6},{8,7},{9,8},{10,9},{11,1... | collective-permute-start | bytes 1572872 | tf_op jit(solution)/shard_map/ppermute | solution.py:23
  178.8 25.1 %collective-permute-start.3 = (f32[2,1,32,2048]{3,2,1,0:T(8,128)S(1)}, f32[2,1,32,2048]{3,2,1,0:T(8,128)S(1)}, u32[]{:S(2)}, u32[]{:S(2)}) collective-permute-start(f32[2,1,32,2048]{3,2,1,0:T(8,128)S(1)} %pad_maximum_fusion.25), channel_id=1, source_target_pairs={{1,0},{2,1},{3,2},{4,3},{5,4},{6,5},{7,6},{8,7},{9,8},{10,9},{11,1... | collective-permute-start | bytes 1572872 | tf_op jit(solution)/shard_map/ppermute | solution.py:23
  181.2 22.7 %collective-permute-start.2 = (f32[2,1,32,2048]{3,2,1,0:T(8,128)S(1)}, f32[2,1,32,2048]{3,2,1,0:T(8,128)S(1)}, u32[]{:S(2)}, u32[]{:S(2)}) collective-permute-start(f32[2,1,32,2048]{3,2,1,0:T(8,128)S(1)} %pad_maximum_fusion.25), channel_id=1, source_target_pairs={{0,1},{1,2},{2,3},{3,4},{4,5},{5,6},{6,7},{7,8},{8,9},{9,10},{10,1... | collective-permute-start | bytes 1572872 | tf_op jit(solution)/shard_map/ppermute | solution.py:21
  219.8 53.6 %all-to-all-start.2 = ((bf16[32,2,6144]{2,1,0:T(2,128)(2,1)}), bf16[32,2,6144]{2,1,0:T(2,128)(2,1)}, u32[]{:S(2)}, u32[]{:S(2)}) async-start(bf16[32,2,6144]{2,1,0:T(2,128)(2,1)} %reshape.1287), calls=%async_computation.2 | async-start | bytes 1572864 | tf_op jit(solution)/shard_map/all_to_all | solution.py:114
  289.3 17.0 %copy-start = (f32[4,1,2,1024,32]{3,4,2,0,1:T(8,128)S(1)}, f32[4,1,2,1024,32]{3,4,2,0,1:T(8,128)}, u32[]{:S(2)}) copy-start(f32[4,1,2,1024,32]{3,4,2,0,1:T(8,128)} %reshape.1253) | copy-start | bytes 3145732
